TPU v7x, 32 devices: a whole 2x2x4 slice. The times are simulated.
32 devices in a mesh: groups: 2 (over y), cols: 4 (over z), tok: 2 (over x), sub: 2 (over core).
Axes of the slice: x: 2, y: 2, z: 4, core: 2. Of those that a mesh axis runs over, the one named last changes fastest.
Arguments:
- tokens: bfloat16 [2048, 8192], P(('groups', 'tok'), 'cols'), parts along dimension 0
- damp_ratio: int32 [2], P('groups'), parts along dimension 0, may hold values from 1 to 10, as said below
- panel_index: int32 [2], P('groups'), parts along dimension 0, may hold values from 0 to 14
Outputs:
- updated: float32 [16384, 8192], P(('groups', 'tok', 'sub'), 'cols'), parts along dimension 0
- panel: float32 [16384, 512], P(('groups', 'tok', 'sub')), parts along dimension 0
There are 2 independent parts, one for each index of `groups`. A program takes and returns all parts, laid end to end along the dimension named above; each array names one. Nothing has to cross between parts.
Inputs may be any that keep to these rules, and one draw needn't show every extreme that they name: `damp_ratio`: every odd-numbered part has the most. `panel_index`: a trailing block always follows the panel.
All inputs are finite; a program needn't handle non-finite values.
Results may differ from a plain program's by a relative error of at most 0.0003.
Values may be sent and summed in bfloat16 or wider, within the bound.
A program may use at most 192 MiB of HBM per device.

v0:
```python
import jax
import jax.numpy as jnp
from jax import lax
from jax.sharding import PartitionSpec as P

D = 8192
PANEL = 512


def from_root(value, axis, source):
    kept = jnp.where(lax.axis_index(axis) == source, value, 0).astype(value.dtype)
    return lax.psum(kept, axis)


def body(tokens, damp_ratio, panel_index):
    tok_rows = tokens.shape[0]
    col_width = tokens.shape[1]
    tok_count = lax.axis_size("tok")
    sub_count = lax.axis_size("sub")
    row_count = D // (tok_count * sub_count)
    sub_rank = lax.axis_index("sub")
    gathered = lax.all_gather(tokens, "cols", axis=1, tiled=True)
    selected = lax.dynamic_index_in_dim(
        gathered.reshape(tok_rows, tok_count, sub_count, row_count), sub_rank, 2, keepdims=False
    )
    selected = selected.reshape(tok_rows, tok_count * row_count)
    gram_block = lax.psum_scatter(
        lax.dot_general(
            selected, tokens, (((0,), (0,)), ((), ())), preferred_element_type=jnp.float32
        ),
        "tok",
        scatter_dimension=0,
        tiled=True,
    ) * (2.0 / (tok_rows * tok_count))
    row_rank = lax.axis_index(("tok", "sub"))
    row_base = row_rank * row_count
    col_base = lax.axis_index("cols") * col_width
    row_index = row_base + jnp.arange(row_count, dtype=jnp.int32)
    col_index = col_base + jnp.arange(col_width, dtype=jnp.int32)
    on_diagonal = row_index[:, None] == col_index[None, :]
    trace_sum = lax.psum(jnp.sum(jnp.where(on_diagonal, gram_block, 0.0)), ("cols", "tok", "sub"))
    damping = damp_ratio[0].astype(jnp.float32) / 100.0 * (trace_sum / D)
    hessian = gram_block + jnp.where(on_diagonal, damping, 0.0)
    panel_start = panel_index[0] * PANEL
    end_col = panel_start + PANEL
    local_width = min(col_width, PANEL)
    local_offset = jnp.clip(panel_start - col_base, 0, col_width - local_width)
    first_col = col_base + local_offset
    owns_piece = (first_col >= panel_start) & (first_col + local_width <= end_col)
    local_piece = jnp.where(
        owns_piece, lax.dynamic_slice_in_dim(hessian, local_offset, local_width, 1), 0.0
    )
    place_at = jnp.clip(first_col - panel_start, 0, PANEL - local_width)
    panel_piece = lax.dynamic_update_slice(
        jnp.zeros((row_count, PANEL), jnp.float32), local_piece, (jnp.int32(0), place_at)
    )
    panel_rows = lax.psum(panel_piece, "cols")
    owner_rank = panel_start // row_count
    row_offset = jnp.clip(panel_start - row_base, 0, row_count - PANEL)
    diagonal_block = lax.dynamic_slice_in_dim(panel_rows, row_offset, PANEL, 0)
    across = lax.dynamic_slice_in_dim(hessian, row_offset, PANEL, 0)
    diagonal_block, across = (
        from_root(diagonal_block, ("tok", "sub"), owner_rank),
        from_root(across, ("tok", "sub"), owner_rank),
    )
    factor = jnp.linalg.cholesky(diagonal_block)
    panel_left = jax.scipy.linalg.solve_triangular(factor, panel_rows.T, lower=True).T
    panel_out = jnp.where(row_index[:, None] >= panel_start, panel_left, 0.0)
    column_side = jax.scipy.linalg.solve_triangular(factor, across, lower=True)
    column_side = jnp.where(col_index[None, :] >= end_col, column_side, 0.0)
    update = jnp.dot(panel_left, column_side, precision=lax.Precision.HIGHEST)
    updated = hessian - jnp.where(row_index[:, None] >= end_col, update, 0.0)
    return (updated, panel_out)


def solution(mesh):
    placed = (P(("groups", "tok"), "cols"), P("groups"), P("groups"))
    return jax.shard_map(
        body,
        mesh=mesh,
        in_specs=placed,
        out_specs=(P(("groups", "tok", "sub"), "cols"), P(("groups", "tok", "sub"), None)),
        check_vma=False,
    )
```

profile of v0, /device:TPU:0, one launch (start us, length us, event | category | flops | bytes accessed | tf_op | source)
XLA Modules:
  0.0 1113.6 jit_solution(15332046235909542102)
XLA Ops:
  7.2 3.9 copy.45
  11.2 152.4 %all-gather.2.cloned.1.call-done = bf16[512,8192]{0,1:T(8,128)(2,1)} async-done(((bf16[512,2048]{0,1:T(8,128)(2,1)}), bf16[512,8192]{0,1:T(8,128)(2,1)}) %all-gather.2.cloned.1.call-update) | async-done | bytes 8388624 | tf_op jit(solution)/shard_map/all_gather | solution.py:22
  163.7 2.6 constant_dynamic-slice_fusion.1
  166.5 15.3 %fusion.71 = f32[4096,2048]{0,1:T(8,128)} fusion(bf16[512,4096]{0,1:T(8,128)(2,1)S(1)} %bitcast.74, bf16[512,2048]{1,0:T(8,128)(2,1)S(1)} %copy-done.11), kind=kOutput, calls=%fused_computation.116 | convolution fusion | flops 8589934592 | bytes 39845888 | tf_op jit(solution)/shard_map/dot_general | solution.py:28
  183.2 365.9 %reduce-scatter.2.cloned.1.call-done = f32[2048,2048]{0,1:T(8,128)} async-done(((f32[4096,2048]{0,1:T(8,128)}), f32[2048,2048]{0,1:T(8,128)}) %reduce-scatter.2.cloned.1.call-update) | async-done | bytes 16777232 | tf_op jit(solution)/shard_map/reduce_scatter | solution.py:27
  549.1 9.0 fusion
  558.1 32.9 %psum.28 = f32[]{:T(128)} all-reduce(f32[]{:T(128)} %fusion), channel_id=1, replica_groups=mesh['groups'=2,'cols'=4,'tok'=2,'sub'=2] {'cols','tok','sub'}, use_global_device_ids=true, to_apply=%region_2.3 | all-reduce | flops 1 | bytes 8 | tf_op jit(solution)/shard_map/psum | solution.py:41
  591.6 7.3 fusion.1
  599.0 6.2 copy-done
  605.1 2.5 dynamic-slice_select_fusion.1
  607.9 5.4 dynamic-slice_select_fusion
  613.3 146.7 %all-reduce.5.cloned.1.call-done = f32[2048,512]{0,1:T(8,128)} async-done(((f32[2048,512]{0,1:T(8,128)}), f32[2048,512]{0,1:T(8,128)}) %all-reduce.5.cloned.1.call-update) | async-done | bytes 4194320 | tf_op jit(solution)/shard_map/psum | solution.py:57
  760.0 2.5 dynamic-slice_select_fusion.2
  762.6 102.2 %all-reduce.7.cloned.1.call-done = (f32[512,2048]{0,1:T(8,128)}, f32[512,512]{0,1:T(8,128)}) async-done(((f32[512,2048]{0,1:T(8,128)}, f32[512,512]{0,1:T(8,128)}), (f32[512,2048]{0,1:T(8,128)}, f32[512,512]{0,1:T(8,128)})) %all-reduce.7.cloned.1.call-update) | async-done | bytes 5242896 | tf_op jit(solution)/shard_map/psum | solution.py:12
  867.9 11.7 %cholesky.103 = f32[128,128]{1,0:T(8,128)S(1)} custom-call(f32[128,128]{1,0:T(8,128)S(1)} %cholesky.263), custom_call_target="Cholesky" | custom-call | tf_op jit(solution)/shard_map/jit(cholesky)/cholesky | solution.py:66
  879.6 9.8 custom-call.30
  890.1 12.1 %cholesky.215 = f32[128,128]{1,0:T(8,128)S(1)} custom-call(f32[128,128]{1,0:T(8,128)S(1)} %cholesky.267), custom_call_target="Cholesky" | custom-call | tf_op jit(solution)/shard_map/jit(cholesky)/cholesky | solution.py:66
  902.6 9.8 custom-call.31
  913.5 11.7 %cholesky.236 = f32[128,128]{1,0:T(8,128)S(1)} custom-call(f32[128,128]{1,0:T(8,128)S(1)} %cholesky.272), custom_call_target="Cholesky" | custom-call | tf_op jit(solution)/shard_map/jit(cholesky)/cholesky | solution.py:66
  925.4 9.8 custom-call.32
  936.0 11.9 %cholesky.253 = f32[128,128]{1,0:T(8,128)S(1)} custom-call(f32[128,128]{1,0:T(8,128)S(1)} %convolution_subtract_fusion.6), custom_call_target="Cholesky" | custom-call | tf_op jit(solution)/shard_map/jit(cholesky)/cholesky | solution.py:66
  953.1 10.5 while.4
  963.6 40.2 %custom-call.34 = f32[4,128,128]{1,2,0:T(8,128)S(1)} custom-call(f32[4,128,128]{2,1,0:T(8,128)} %get-tuple-element.17), custom_call_target="InvertDiagBlocksLowerTriangular" | custom-call | tf_op jit(solution)/shard_map/jit(_solve_triangular)/triangular_solve | solution.py:67
  1013.8 4.0 fusion.23
  1022.0 2.4 fusion.34
  1024.5 3.1 convolution_subtract_fusion.2
  1028.7 4.8 convolution_subtract_fusion
  1035.6 7.2 fusion.20
  1042.8 2.5 copy.66
  1048.1 3.1 fusion.59
  1057.0 32.3 %select_subtract_fusion = f32[2048,2048]{0,1:T(8,128)} fusion(f32[2048,2048]{0,1:T(8,128)} %copy-done, pred[2048]{0:T(1024)(128)(4,1)S(1)} %get-tuple-element.69, f32[128,2048]{0,1:T(8,128)S(1)} %fusion.58, f32[128,2048]{0,1:T(8,128)S(1)} %copy-done.7, f32[128,2048]{0,1:T(8,128)S(1)} %copy-done.8, f32[128,2048]{0,1:T(8,128)S(1)} %copy-done.9, ...), kind=kOutput, calls=%fused_computation.6 | convolution fusion | flops 25785532416 | bytes 41947136 | tf_op jit(solution)/shard_map/dot_general | solution.py:71
  1089.3 17.6 %copy.69 = f32[2048,2048]{1,0:T(8,128)} copy(f32[2048,2048]{0,1:T(8,128)} %select_subtract_fusion) | data formatting | bytes 33554432
  (101 shorter events, 45.8 us)
Async XLA Ops:
  7.2 156.5 %all-gather.2.cloned.1.call-start = ((), (), s32[]{:S(2)}) async-start(), calls=%async_computation.1 | async-start | bytes 10485760 | tf_op jit(solution)/shard_map/all_gather | solution.py:22
  11.2 537.9 %reduce-scatter.2.cloned.1.call-start = ((), (), s32[]{:S(2)}) async-start(), calls=%async_computation.2 | async-start | bytes 50331648 | tf_op jit(solution)/shard_map/reduce_scatter | solution.py:27
  163.7 2.9 copy-start.11
  181.8 578.2 %all-reduce.5.cloned.1.call-start = ((), (), s32[]{:S(2)}) async-start(), calls=%async_computation.3 | async-start | bytes 8388608 | tf_op jit(solution)/shard_map/psum | solution.py:57
  599.0 6.2 copy-start
  607.6 257.2 %all-reduce.7.cloned.1.call-start = ((), (), s32[]{:S(2)}) async-start(), calls=%async_computation.4 | async-start | bytes 10485760 | tf_op jit(solution)/shard_map/psum | solution.py:12
  963.6 42.6 %copy-start.6 = (f32[512,512]{0,1:T(8,128)}, f32[512,512]{0,1:T(8,128)S(1)}, u32[]{:S(2)}) copy-start(f32[512,512]{0,1:T(8,128)S(1)} %get-tuple-element.132) | copy-start | bytes 3145732
  1003.8 5.8 copy-start.5
  1012.8 1.0 copy-start.4
  1022.0 6.6 copy-start.10
  1034.6 1.0 copy-start.3
  1046.7 6.8 copy-start.1
  1048.1 5.5 copy-start.2
  1053.6 2.4 copy-start.7
  1053.6 2.4 copy-start.8
  1053.6 3.4 copy-start.9
Sparse Core Ops, SparseCore 0:
  11.3 152.3 all-gather.1
  181.9 367.0 reduce-scatter.1
  607.8 152.2 all-reduce.4
  763.1 101.7 all-reduce.6
where the time goes:
time: 1120 us; the launch traced here: 1110 us
  waiting for transfers between devices  767 us (68%)
  other arithmetic  150 us (13%)
  matrix products  88 us (8%)
  local copies, waits for them, and re-layouts  55.7 us (5%)
  blocking collectives  32.9 us (3%)
  between operations  18.8 us (2%)
    reduce_scatter x1, waiting for transfers between devices, body(): lax.psum_scatter(lax.dot_general(selected, tokens, (((0,), (0,)), ((), ()...  366 us
    all_gather x1, waiting for transfers between devices, body(): gathered = lax.all_gather(tokens, 'cols', axis=1, tiled=True)  152 us
    psum x1, waiting for transfers between devices, body(): panel_rows = lax.psum(panel_piece, 'cols')  147 us
    psum x1, waiting for transfers between devices, from_root(): return lax.psum(kept, axis)  102 us
    another operation x15, other arithmetic, body(): factor = jnp.linalg.cholesky(diagonal_block)  79.5 us
    another operation x4, other arithmetic, body(): jax.scipy.linalg.solve_triangular(factor, panel_rows.T, lower=True)  40.3 us
    psum x1, blocking collectives, body(): lax.psum(jnp.sum(jnp.where(on_diagonal, gram_block, 0.0)), ('cols', 'tok'...  32.9 us
    dot_general x1, matrix products, body(): update = jnp.dot(panel_left, column_side, precision=lax.Precision.HIGHEST)  32.3 us
  transfers between devices with their start and end apart: 4, of which 4 were waited for; matrix products, arithmetic and copies ran while one was open for 0% of the time, Pallas kernels for 0%

commit v1 on v0

v1 whole, which is shorter than its diff:
```python
import jax
import jax.numpy as jnp
from jax import lax
from jax.experimental import pallas as pl
from jax.experimental.pallas import tpu as pltpu
from jax.sharding import PartitionSpec as P

D = 8192
PANEL = 512
BLOCK = 128
GROUP = 4


def exact_dot(a, b, contract):
    return lax.dot_general(
        a, b, (contract, ((), ())), precision=lax.Precision.HIGHEST, preferred_element_type=jnp.float32
    )


def eliminate(a):
    n = a.shape[0]
    row = lax.broadcasted_iota(jnp.int32, (n, n), 0)
    col = lax.broadcasted_iota(jnp.int32, (n, n), 1)
    left, right = a, jnp.where(row == col, 1.0, 0.0).astype(jnp.float32)
    top = 0
    upper, inverse = [], []
    for start in range(0, n, GROUP):
        columns = [
            jnp.broadcast_to(left[:, start + j : start + j + 1], left.shape) for j in range(GROUP)
        ]
        rows = top + lax.broadcasted_iota(jnp.int32, left.shape, 0)
        for j in range(GROUP):
            k = start + j
            at = k - top
            scale = lax.rsqrt(columns[j][at : at + 1, :])
            upper.append(left[at : at + 1, :] * scale)
            inverse.append(right[at : at + 1, :] * scale)
            if k == n - 1:
                break
            multiplier = jnp.where(rows > k, columns[j] * scale, 0.0)
            for later in range(j + 1, GROUP):
                columns[later] = columns[later] - multiplier * (columns[later][at : at + 1, :] * scale)
            left = left - multiplier * upper[-1]
            right = right - multiplier * inverse[-1]
        if (start + GROUP) % 8 == 0 and start + GROUP < n:
            done = start + GROUP - top
            left, right, top = left[done:, :], right[done:, :], start + GROUP
    return jnp.concatenate(upper, 0), jnp.concatenate(inverse, 0)


def factor_kernel(block_ref, factor_ref, inverse_ref, rest_ref):
    n = block_ref.shape[0]
    b = BLOCK
    rest_ref[...] = block_ref[...]
    factor_ref[...] = jnp.zeros_like(factor_ref)
    inverse_ref[...] = jnp.zeros_like(inverse_ref)
    row = lax.broadcasted_iota(jnp.int32, (b, b), 0)
    col = lax.broadcasted_iota(jnp.int32, (b, b), 1)
    for o in range(0, n, b):
        e = o + b
        upper, inverse = eliminate(rest_ref[o:e, o:e])
        factor_ref[o:e, o:e] = jnp.where(row <= col, upper, 0.0).T
        inverse_ref[o:e, o:e] = inverse
        if e < n:
            below = exact_dot(rest_ref[e:, o:e], inverse, ((1,), (1,)))
            factor_ref[e:, o:e] = below
            rest_ref[e:, e:] = rest_ref[e:, e:] - exact_dot(below, below, ((1,), (1,)))
        if o:
            crossed = exact_dot(factor_ref[o:e, :o], inverse_ref[:o, :o], ((1,), (0,)))
            inverse_ref[o:e, :o] = -exact_dot(inverse, crossed, ((1,), (0,)))


def factor_and_inverse(block):
    shape = jax.ShapeDtypeStruct(block.shape, jnp.float32)
    return pl.pallas_call(
        factor_kernel,
        out_shape=[shape, shape],
        in_specs=[pl.BlockSpec(memory_space=pltpu.VMEM)],
        out_specs=[pl.BlockSpec(memory_space=pltpu.VMEM)] * 2,
        scratch_shapes=[pltpu.VMEM(block.shape, jnp.float32)],
        compiler_params=pltpu.CompilerParams(vmem_limit_bytes=32 << 20),
        cost_estimate=pl.CostEstimate(flops=10**9, bytes_accessed=4 << 20, transcendentals=0),
        name="factor",
    )(block)


def split_bf16(x, count):
    parts = []
    for _ in range(count):
        high = lax.reduce_precision(x, 8, 7)
        parts.append(high.astype(jnp.bfloat16))
        x = x - high
    return parts


def dot_bf16(a, b, contract):
    return lax.dot_general(a, b, (contract, ((), ())), preferred_element_type=jnp.float32)


def gather_tokens(tokens):
    half = tokens.shape[0] // lax.axis_size("sub")
    mine = lax.dynamic_slice_in_dim(tokens, lax.axis_index("sub") * half, half, 0)
    pieces = lax.all_gather(mine, ("cols", "tok", "sub"))
    return pieces.reshape(lax.axis_size("cols"), -1, tokens.shape[1])


def body(tokens, damp_ratio, panel_index):
    col_width = tokens.shape[1]
    row_count = D // (lax.axis_size("tok") * lax.axis_size("sub"))
    total = tokens.shape[0] * lax.axis_size("tok")
    scale = 2.0 / total
    row_rank = lax.axis_index(("tok", "sub"))
    col_rank = lax.axis_index("cols")
    row_index = row_rank * row_count + jnp.arange(row_count, dtype=jnp.int32)
    col_index = col_rank * col_width + jnp.arange(col_width, dtype=jnp.int32)

    squares = jnp.sum(jnp.square(tokens.astype(jnp.float32)))
    trace = lax.psum(squares, ("cols", "tok")) * scale
    damping = damp_ratio[0].astype(jnp.float32) / 100.0 * (trace / D)

    blocks = gather_tokens(tokens)
    start = panel_index[0] * PANEL
    end = start + PANEL

    def columns(first, width):
        if width <= col_width:
            block = lax.dynamic_index_in_dim(blocks, first // col_width, 0, keepdims=False)
            if width == col_width:
                return block
            return lax.dynamic_slice_in_dim(block, first % col_width, width, 1)
        several = lax.dynamic_slice_in_dim(blocks, first // col_width, width // col_width, 0)
        return jnp.swapaxes(several, 0, 1).reshape(total, width)

    own_rows = columns(row_rank * row_count, row_count)
    own_cols = columns(col_rank * col_width, col_width)
    in_panel = columns(start, PANEL)

    square = dot_bf16(in_panel, in_panel, ((0,), (0,))) * scale
    square = square + damping * jnp.eye(PANEL, dtype=jnp.float32)
    factor, inverse = factor_and_inverse(square)

    lead = sum(dot_bf16(part, in_panel, ((1,), (1,))) for part in split_bf16(inverse, 3)) * scale
    lead_high, lead_low = split_bf16(lead, 2)

    def solved(x):
        return dot_bf16(lead_high, x, ((1,), (0,))) + dot_bf16(lead_low, x, ((1,), (0,)))

    rows_solved = solved(own_rows)
    cols_solved = solved(own_cols)
    panel_out = jnp.where(row_index[:, None] >= end, rows_solved.T, 0.0)
    offset = start - row_rank * row_count
    holds = (offset >= 0) & (offset < row_count)
    offset = jnp.clip(offset, 0, row_count - PANEL)
    kept = lax.dynamic_slice_in_dim(panel_out, offset, PANEL, 0)
    panel_out = lax.dynamic_update_slice_in_dim(panel_out, jnp.where(holds, factor, kept), offset, 0)

    row_high, row_low = split_bf16(jnp.where(row_index[None, :] >= end, rows_solved, 0.0), 2)
    col_high, col_low = split_bf16(jnp.where(col_index[None, :] >= end, cols_solved * (-1.0 / scale), 0.0), 2)
    left = jnp.concatenate([own_rows, row_high, row_high, row_low], 0)
    right = jnp.concatenate([own_cols, col_high, col_low, col_high], 0)
    updated = dot_bf16(left, right, ((0,), (0,))) * scale
    updated = updated + jnp.where(row_index[:, None] == col_index[None, :], damping, 0.0)
    return (updated, panel_out)


def solution(mesh):
    placed = (P(("groups", "tok"), "cols"), P("groups"), P("groups"))
    return jax.shard_map(
        body,
        mesh=mesh,
        in_specs=placed,
        out_specs=(P(("groups", "tok", "sub"), "cols"), P(("groups", "tok", "sub"), None)),
        check_vma=False,
    )
```

time: 1120 us -> 263 us (0.23)
  waiting for transfers between devices: 767 us -> 103 us
  other arithmetic: 150 us -> 12.7 us
  matrix products: 88 us -> 56.6 us
  local copies, waits for them, and re-layouts: 55.7 us -> 28.2 us
  Pallas kernels: 0 us -> 20.9 us
    reduce_scatter x1 -> x0, waiting for transfers between devices: 366 us -> none  [body(): lax.psum_scatter(lax.dot_general(selected, tokens, (((0,), (0,)), ((), ()...]
    psum x2 -> x0, waiting for transfers between devices: 249 us -> none  [the longest x1 147 us: body(): panel_rows = lax.psum(panel_piece, 'cols')]
    another operation x19 -> x0, other arithmetic: 120 us -> none  [the longest x15 79.5 us: body(): factor = jnp.linalg.cholesky(diagonal_block)]
    all_gather x1, waiting for transfers between devices: 152 us -> 103 us  [gather_tokens(): pieces = lax.all_gather(mine, ('cols', 'tok', 'sub'))]
    another operation x20 -> x0, matrix products: 40.4 us -> none  [the longest x7 22.1 us: body(): column_side = jax.scipy.linalg.solve_triangular(factor, across, lower=True)]
    unnamed x26 -> x10, local copies, waits for them, and re-layouts: 30.9 us -> 0.02 us
    pallas_call x0 -> x1, Pallas kernels: none -> 20.9 us  [factor_and_inverse(): pl.pallas_call(factor_kernel, out_shape=[shape, shape], in_specs=[pl.Bloc...]
    another operation x40 -> x0, local copies, waits for them, and re-layouts: 20.6 us -> none  [the longest x24 14.7 us: body(): jax.scipy.linalg.solve_triangular(factor, panel_rows.T, lower=True)]
  transfers between devices with their start and end apart: 4 -> 1, of which waited for: 4 -> 1; matrix products, arithmetic and copies ran while one was open for 0% -> 1% of each run, Pallas kernels for 0% -> 0%
where the time goes in v1:
time: 263 us; the launch traced here: 262 us
  waiting for transfers between devices  103 us (39%)
  matrix products  56.6 us (22%)
  local copies, waits for them, and re-layouts  28.2 us (11%)
  blocking collectives  24 us (9%)
  Pallas kernels  20.9 us (8%)
  between operations  16.1 us (6%)
  other arithmetic  12.7 us (5%)
    all_gather x1, waiting for transfers between devices, gather_tokens(): pieces = lax.all_gather(mine, ('cols', 'tok', 'sub'))  103 us
    dot_general x9, matrix products, dot_bf16(): lax.dot_general(a, b, (contract, ((), ())), preferred_element_type=jnp.fl...  56.6 us
    psum x1, blocking collectives, body(): trace = lax.psum(squares, ('cols', 'tok')) * scale  24 us
    pallas_call x1, Pallas kernels, factor_and_inverse(): pl.pallas_call(factor_kernel, out_shape=[shape, shape], in_specs=[pl.Bloc...  20.9 us
    convert_element_type x4, local copies, waits for them, and re-layouts, split_bf16(): parts.append(high.astype(jnp.bfloat16))  14.8 us
    dot_general x1, other arithmetic, dot_bf16(): lax.dot_general(a, b, (contract, ((), ())), preferred_element_type=jnp.fl...  9.54 us
    squeeze x1, local copies, waits for them, and re-layouts, columns(): lax.dynamic_index_in_dim(blocks, first // col_width, 0, keepdims=False)  7.41 us
  transfers between devices with their start and end apart: 1, of which 1 were waited for; matrix products, arithmetic and copies ran while one was open for 1% of the time, Pallas kernels for 0%

profile of v1, /device:TPU:0, one launch (start us, length us, event | category | flops | bytes accessed | tf_op | source)
XLA Modules:
  0.0 261.6 jit_solution(7158435037931149925)
XLA Ops:
  7.2 0.0 copy-start.1
  7.2 0.0 all-gather.3.cloned.1.call-start
  7.2 2.4 constant_dynamic-slice_fusion
  9.7 0.0 all-gather.3.cloned.1.call-update
  9.7 0.0 copy-done.1
  9.7 1.7 multiply_reduce_fusion
  11.4 24.0 %psum.7 = f32[]{:T(128)} all-reduce(f32[]{:T(128)} %multiply_reduce_fusion), channel_id=1, replica_groups=mesh['groups'=2,'cols'=4,'tok'=2,'sub'=2] {'cols','tok'}, use_global_device_ids=true, to_apply=%region_1.0 | all-reduce | flops 1 | bytes 8 | tf_op jit(solution)/shard_map/psum | solution.py:118
  37.3 103.2 %all-gather.3.cloned.1.call-done = bf16[4096,2048]{1,0:T(8,128)(2,1)} async-done(((bf16[256,2048]{1,0:T(8,128)(2,1)}), bf16[4096,2048]{1,0:T(8,128)(2,1)}) %all-gather.3.cloned.1.call-update) | async-done | bytes 16777232 | tf_op jit(solution)/shard_map/all_gather | solution.py:103
  140.5 2.8 %fusion.23.block_ref = f32[512,512]{1,0:T(8,128)S(1)} fusion(bf16[4,1024,2048]{2,1,0:T(8,128)(2,1)} %bitcast.24, s32[]{:T(128)S(6)} %select_n.68, s32[]{:T(128)S(6)} %select_n.71, f32[]{:T(128)S(6)} %mul.68), kind=kOutput, calls=%fused_computation.39 | convolution fusion | flops 537919488 | bytes 2097164 | tf_op jit(solution)/shard_map/dot_general | solution.py:97
  143.3 20.9 %factor.1 = (f32[512,512]{1,0:T(8,128)S(1)}, f32[512,512]{1,0:T(8,128)S(1)}) custom-call(f32[512,512]{1,0:T(8,128)S(1)} %fusion.23.block_ref), custom_call_target="tpu_custom_call" | custom-call | flops 1000000000 | bytes 4194304 | tf_op jit(solution)/shard_map/factor/pallas_call | solution.py:75
  164.2 2.1 fusion.27
  166.3 2.1 fusion.29
  168.4 2.1 add_multiply_fusion
  170.5 0.0 copy-start.3
  170.5 7.4 %dynamic-slice_bitcast_fusion = (bf16[1024,2048]{1,0:T(8,128)(2,1)S(1)}, bf16[1024,2048]{1,0:T(8,128)(2,1)}) fusion(bf16[4,1024,2048]{2,1,0:T(8,128)(2,1)} %bitcast.28, s32[]{:T(128)S(6)} %select_n.74, s32[]{:T(128)S(6)} %select_n.65), kind=kLoop, calls=%fused_computation.25 | loop fusion | bytes 16777224 | tf_op jit(solution)/shard_map/jit(dynamic_index_in_dim)/squeeze | solution.py:127
  177.9 0.0 copy-start
  177.9 2.4 fusion.37
  180.3 0.0 copy-done.3
  180.3 0.0 copy-done
  180.3 4.4 %fusion.20 = (bf16[512,2048]{0,1:T(8,128)(2,1)}, bf16[512,2048]{0,1:T(8,128)(2,1)}) fusion(f32[512,2048]{0,1:T(8,128)S(1)} %fusion.37, bf16[1024,2048]{1,0:T(8,128)(2,1)S(1)} %get-tuple-element.6, f32[512,1024]{1,0:T(8,128)S(1)} %add_multiply_fusion, pred[2048]{0:T(1024)(128)(4,1)S(1)} %get-tuple-element.13), kind=kOutput, calls=%fused_computation.23 | convolution fusion | flops 2157969408 | bytes 14682112 | tf_op jit(solution)/shard_map/dot_general | solution.py:97
  184.7 2.9 %copy.13 = bf16[512,2048]{1,0:T(8,128)(2,1)S(1)} copy(bf16[512,2048]{0,1:T(8,128)(2,1)} %get-tuple-element.8) | data formatting | bytes 4194304 | tf_op jit(solution)/shard_map/convert_element_type | solution.py:91
  187.7 4.0 %copy.12 = bf16[512,2048]{1,0:T(8,128)(2,1)} copy(bf16[512,2048]{0,1:T(8,128)(2,1)} %get-tuple-element.9) | data formatting | bytes 4194304 | tf_op jit(solution)/shard_map/convert_element_type | solution.py:91
  191.6 5.4 %fusion.38 = f32[512,2048]{0,1:T(8,128)S(1)} fusion(bf16[1024,2048]{1,0:T(8,128)(2,1)} %get-tuple-element.7, f32[512,1024]{1,0:T(8,128)} %copy-done.3), kind=kOutput, calls=%fused_computation.55 | convolution fusion | flops 2148532224 | bytes 10485760 | tf_op jit(solution)/shard_map/dot_general | solution.py:97
  197.0 0.0 copy-done.2
  197.0 0.0 copy-done.4
  197.0 4.9 %reduce-precision_convert_fusion.1 = (bf16[512,2048]{0,1:T(8,128)(2,1)}, bf16[512,2048]{0,1:T(8,128)(2,1)}, f32[512,2048]{0,1:T(8,128)}) fusion(f32[512,2048]{0,1:T(8,128)S(1)} %fusion.38, bf16[1024,2048]{1,0:T(8,128)(2,1)S(1)} %copy-done.2, f32[512,1024]{1,0:T(8,128)S(1)} %copy-done.4, pred[2048]{0:T(1024)(128)(4,1)S(1)} %get-tuple-element.14), kind=kOutput, calls=%fused_computation.19 | convolution fusion | flops 2156920832 | bytes 18876416 | tf_op jit(solution)/shard_map/dot_general | solution.py:97
  201.9 4.0 %copy.7 = bf16[512,2048]{1,0:T(8,128)(2,1)} copy(bf16[512,2048]{0,1:T(8,128)(2,1)} %get-tuple-element.10) | data formatting | bytes 4194304 | tf_op jit(solution)/shard_map/convert_element_type | solution.py:91
  205.8 3.9 %copy.9 = bf16[512,2048]{1,0:T(8,128)(2,1)} copy(bf16[512,2048]{0,1:T(8,128)(2,1)} %get-tuple-element.11) | data formatting | bytes 4194304 | tf_op jit(solution)/shard_map/convert_element_type | solution.py:91
  209.8 9.5 %fusion.56 = bf16[2560,2048]{1,0:T(8,128)(2,1)} fusion(bf16[512,2048]{1,0:T(8,128)(2,1)} %copy.12, bf16[512,2048]{1,0:T(8,128)(2,1)S(1)} %copy.13, bf16[1024,2048]{1,0:T(8,128)(2,1)} %copy-done), kind=kLoop, calls=%fused_computation.9.clone.2 | loop fusion | flops 41943040 | bytes 18874368 | tf_op jit(solution)/shard_map/dot_general | solution.py:97
  219.3 1.5 bitcast_select_fusion
  220.8 3.5 %dynamic_update_slice.3 = f32[2048,512]{1,0:T(8,128)} dynamic-update-slice(f32[2048,512]{1,0:T(8,128)} %bitcast.29, f32[512,512]{1,0:T(8,128)S(1)} %bitcast_select_fusion, s32[]{:T(128)S(6)} %min.4, s32[]{:T(128)} %constant.87.clone.1) | dynamic-update-slice | bytes 2097156 | tf_op jit(solution)/shard_map/dynamic_update_slice | solution.py:155
  224.3 30.5 %select_add_fusion = f32[2048,2048]{1,0:T(8,128)} fusion(bf16[512,2048]{1,0:T(8,128)(2,1)} %copy.9, bf16[512,2048]{1,0:T(8,128)(2,1)} %copy.7, bf16[1024,2048]{1,0:T(8,128)(2,1)} %get-tuple-element.7, f32[]{:T(128)S(6)} %mul.68, s32[2048]{0:T(1024)S(1)} %get-tuple-element.15, s32[2048]{0:T(1024)S(1)} %get-tuple-element.16, bf16[2560,2048]{1,0:T(8,128)(2,1)} %fusion.56), kind=kOutput, calls=%fused_computation | convolution fusion | flops 21533556736 | bytes 35667972 | tf_op jit(solution)/shard_map/dot_general | solution.py:97
  (4 shorter events, 0.0 us)
Async XLA Ops:
  7.2 2.5 copy-start.1
  7.2 133.3 %all-gather.3.cloned.1.call-start = ((), (), s32[]{:S(2)}) async-start(), calls=%async_computation | async-start | bytes 17825792 | tf_op jit(solution)/shard_map/all_gather | solution.py:103
  170.5 9.8 %copy-start.3 = (f32[512,1024]{1,0:T(8,128)}, f32[512,1024]{1,0:T(8,128)S(1)}, u32[]{:S(2)}) copy-start(f32[512,1024]{1,0:T(8,128)S(1)} %add_multiply_fusion) | copy-start | bytes 6291460
  177.9 2.4 copy-start
  191.6 5.4 %copy-start.2 = (bf16[1024,2048]{1,0:T(8,128)(2,1)S(1)}, bf16[1024,2048]{1,0:T(8,128)(2,1)}, u32[]{:S(2)}) copy-start(bf16[1024,2048]{1,0:T(8,128)(2,1)} %get-tuple-element.7) | copy-start | bytes 12582916
  191.6 5.4 %copy-start.4 = (f32[512,1024]{1,0:T(8,128)S(1)}, f32[512,1024]{1,0:T(8,128)}, u32[]{:S(2)}) copy-start(f32[512,1024]{1,0:T(8,128)} %copy-done.3) | copy-start | bytes 6291460
Sparse Core Ops, SparseCore 0:
  10.7 129.6 all-gather.2
